TPU v7x, 32 devices: a whole 2x2x4 slice. The times are simulated.
32 devices in a mesh: gx: 4 (over y, x), gy: 8 (over z, core).
Axes of the slice: x: 2, y: 2, z: 4, core: 2. Of those that a mesh axis runs over, the one named last changes fastest.
Arguments:
- right_side: float32 [3, 16, 64, 128], P(None, 'gx', 'gy'), may hold values from -8 to 8
- stiffness: float32 [16, 64, 128], P('gx', 'gy'), may hold values from 2.5 to 25
- panels: float32 [64, 3, 16, 64, 128], P(None, None, 'gx', 'gy'), may hold values from -0.21 to 0.21
Outputs:
- solution: float32 [3, 16, 64, 128], P(None, 'gx', 'gy')
- residual: float32 [3, 16, 64, 128], P(None, 'gx', 'gy')
- coupling: float32 [4, 8, 8, 4096], P('gx', 'gy')
All inputs are finite; a program needn't handle non-finite values.
Results may differ from a plain program's by a relative error of at most 0.0003.
Values sent between devices are 32-bit elements; how exact they have to be, the bound alone decides.
A program may use at most 192 MiB of HBM per device.

v0:
```python
import functools

import jax
import jax.numpy as jnp
from jax import lax
from jax.experimental import pallas as pl
from jax.experimental.pallas import tpu as pltpu
from jax.sharding import PartitionSpec as P

SWEEPS = 4
MESH = pl.DeviceIdType.MESH
mixing = 0.25
damping = 0.5
neighbours = ((-1, -1), (-1, 0), (-1, 1), (0, -1), (0, 1), (1, -1), (1, 0), (1, 1))
ROUNDS = 8


def shift_z(value, step):
    axis = value.ndim - 1
    size = value.shape[axis]
    rolled = pltpu.roll(value, (-step) % size, axis)
    lane = lax.broadcasted_iota(jnp.int32, value.shape, axis)
    edge = size - 1 if step == 1 else 0
    return jnp.where(lane == edge, 0.0, rolled)


def shift_lead(value, step, axis):
    size = value.shape[axis]
    zero = jnp.zeros_like(lax.slice_in_dim(value, 0, 1, axis=axis))
    if step == 1:
        return jnp.concatenate([lax.slice_in_dim(value, 1, size, axis=axis), zero], axis=axis)
    return jnp.concatenate([zero, lax.slice_in_dim(value, 0, size - 1, axis=axis)], axis=axis)


def stencil(field, start, count):
    def planes(c, step):
        return field[c, start + step : start + step + count]

    def up(v):
        return pltpu.roll(v, 15, 1)

    def down(v):
        return pltpu.roll(v, 1, 1)

    low = [planes(c, -1) for c in range(3)]
    mid = [planes(c, 0) for c in range(3)]
    high = [planes(c, 1) for c in range(3)]
    box = []
    for c in range(3):
        along = low[c] + mid[c] + high[c]
        box.append(along + up(along) + down(along))
    dx0, dx1, dx2 = (high[c] - low[c] for c in range(3))
    dy1 = up(mid[1]) - down(mid[1])
    dz2 = shift_z(mid[2], 1) - shift_z(mid[2], -1)
    side0 = mixing * dx2
    out0 = (
        mixing * (up(dx1) - down(dx1)) - box[0] + shift_z(side0 - box[0], 1) - shift_z(side0 + box[0], -1)
    )
    side1 = mixing * (dx0 + dz2)
    out1 = up(side1) - down(side1) - box[1] - shift_z(box[1], 1) - shift_z(box[1], -1)
    side2 = mixing * (dx0 + dy1)
    out2 = shift_z(side2 - box[2], 1) - shift_z(side2 + box[2], -1) - box[2]
    return out0, out1, out2


def ring_image(edge, sx, sy):
    boxes = []
    for c in range(3):
        v = edge[c]
        if sx == 0 or sy == 0:
            v = v + shift_lead(v, 1, 0) + shift_lead(v, -1, 0)
        boxes.append(v + shift_z(v, 1) + shift_z(v, -1))
    if sx and sy:
        return [mixing * sx * sy * edge[1] - boxes[0], mixing * sx * sy * edge[0] - boxes[1], -boxes[2]]

    def along(v):
        return shift_lead(v, 1, 0) - shift_lead(v, -1, 0)

    def third(v):
        return shift_z(v, 1) - shift_z(v, -1)

    if sx:
        return [
            -mixing * sx * (along(edge[1]) + third(edge[2])) - boxes[0],
            -mixing * sx * along(edge[0]) - boxes[1],
            -mixing * sx * third(edge[0]) - boxes[2],
        ]
    return [
        -mixing * sy * along(edge[1]) - boxes[0],
        -mixing * sy * (along(edge[0]) + third(edge[2])) - boxes[1],
        -mixing * sy * third(edge[1]) - boxes[2],
    ]


def split_rows(value):
    high = value.astype(jnp.bfloat16)
    low = (value - high.astype(jnp.float32)).astype(jnp.bfloat16)
    return jnp.concatenate([high, low], axis=0)


def kernel(
    n_gx, n_gy, r_ref, s_ref, z_ref, x_out, res_out, tile_out,
    panel, far_x, far_y, far_c, image_x, send, recv, ext, ext_r, ext_inv, own_p, own_z, own_w, own_v, own_u,
    weight, coarse, dots, sums_x, sums_y,
    send_sem, recv_sem, far_send, far_recv, sx_send, sx_recv, sy_send, sy_recv,
):
    X, Y, Z = s_ref.shape
    K = panel.shape[3]
    rows = 3 * X * Y
    gx, gy = lax.axis_index("gx"), lax.axis_index("gy")

    def exists(d):
        sx, sy = neighbours[d]
        ok = jnp.bool_(True)
        if sx < 0:
            ok = gx > 0
        if sx > 0:
            ok = gx < n_gx - 1
        if sy:
            ok_y = gy > 0 if sy < 0 else gy < n_gy - 1
            ok = jnp.logical_and(ok, ok_y) if sx else ok_y
        return ok

    def peer(d):
        return (gx + neighbours[d][0], gy + neighbours[d][1])

    recv[...] = jnp.zeros_like(recv)
    ext[...] = jnp.zeros_like(ext)
    ext_r[...] = jnp.zeros_like(ext_r)
    ext_inv[...] = jnp.zeros_like(ext_inv)
    dots[...] = jnp.zeros_like(dots)
    barrier = pltpu.get_barrier_semaphore()
    count = jnp.int32(n_gx - 1 + n_gy - 1)
    for o in range(1, n_gx):
        pl.semaphore_signal(barrier, inc=1, device_id=(lax.rem(gx + o, n_gx), gy), device_id_type=MESH)
    for o in range(1, n_gy):
        pl.semaphore_signal(barrier, inc=1, device_id=(gx, lax.rem(gy + o, n_gy)), device_id_type=MESH)
    for d in (0, 2, 5, 7):
        count = count + exists(d).astype(jnp.int32)

        @pl.when(exists(d))
        def _():
            pl.semaphore_signal(barrier, inc=1, device_id=peer(d), device_id_type=MESH)

    pl.semaphore_wait(barrier, count)

    def length(d, with_stiff):
        sx, sy = neighbours[d]
        if sx and sy:
            return 8
        if sx:
            return 32 if with_stiff else 24
        return 16

    def message(turn, d):
        n = length(d, turn == 0)
        return pltpu.make_async_remote_copy(
            src_ref=send.at[turn, d, 0:n],
            dst_ref=recv.at[turn, 7 - d, 0:n],
            send_sem=send_sem.at[turn, d],
            recv_sem=recv_sem.at[turn, 7 - d],
            device_id=peer(d),
            device_id_type=MESH,
        )

    def arrival(turn, d):
        n = length(d, turn == 0)
        return pltpu.make_async_remote_copy(
            src_ref=send.at[turn, d, 0:n],
            dst_ref=recv.at[turn, d, 0:n],
            send_sem=send_sem.at[turn, d],
            recv_sem=recv_sem.at[turn, d],
            device_id=peer(d),
            device_id_type=MESH,
        )

    def launch(turn):
        for d in range(8):

            @pl.when(exists(d))
            def _():
                message(turn, d).start()

    def await_all(turn):
        for d in range(8):

            @pl.when(exists(d))
            def _():
                arrival(turn, d).wait_recv()

    def pack_own(turn, field):
        for d, (sx, sy) in enumerate(neighbours):
            px, py = (0 if sx < 0 else X - 1), (0 if sy < 0 else Y - 1)
            for c in range(3):
                if sx and sy:
                    send[turn, d, c, :] = field[c, px, py, :]
                elif sx:
                    send[turn, d, c * Y : (c + 1) * Y, :] = field[c, px]
                else:
                    for x in range(X):
                        send[turn, d, c * X + x, :] = field[c, x, py, :]

    def pack_ring(turn):
        for d, (sx, sy) in enumerate(neighbours):
            px, py = (1 if sx < 0 else X + 2), (15 if sy < 0 else 8)
            for c in range(3):
                if sx and sy:
                    send[turn, d, c, :] = ext[c, px, py, :]
                elif sx:
                    send[turn, d, c * Y : (c + 1) * Y, :] = ext[c, px, 0:Y]
                else:
                    for x in range(X):
                        send[turn, d, c * X + x, :] = ext[c, 2 + x, py, :]

    def unpack_halo(turn, target):
        for d, (sx, sy) in enumerate(neighbours):
            px, py = (1 if sx < 0 else X + 2), (15 if sy < 0 else 8)
            for c in range(3):
                if sx and sy:
                    target[c, px, py, :] = recv[turn, d, c, :]
                elif sx:
                    target[c, px, 0:Y] = recv[turn, d, c * Y : (c + 1) * Y, :]
                else:
                    for x in range(X):
                        target[c, 2 + x, py, :] = recv[turn, d, c * X + x, :]

    def add_ring(turn, target):
        for d, (sx, sy) in enumerate(neighbours):
            px, py = (0 if sx < 0 else X - 1), (0 if sy < 0 else Y - 1)
            for c in range(3):
                if sx and sy:
                    target[c, px, py, :] += recv[turn, d, c, :]
                elif sx:
                    target[c, px] += recv[turn, d, c * Y : (c + 1) * Y, :]
                else:
                    for x in range(X):
                        target[c, x, py, :] += recv[turn, d, c * X + x, :]

    pack_own(0, r_ref)
    for d, (sx, sy) in enumerate(neighbours):
        px, py = (0 if sx < 0 else X - 1), (0 if sy < 0 else Y - 1)
        if sx and sy:
            send[0, d, 3, :] = s_ref[px, py, :]
        elif sx:
            send[0, d, 3 * Y : 4 * Y, :] = s_ref[px]
        else:
            for x in range(X):
                send[0, d, 3 * X + x, :] = s_ref[x, py, :]
    launch(0)

    def relayout(y, carry):
        for c in range(3):
            for x in range(X):
                for t in range(K // 8):
                    row = (c * X + x) * Y + y + t * 8 * rows
                    panel[c, x, y, t * 8 : t * 8 + 8, :] = z_ref[pl.ds(row, 8, stride=rows), :]
        return carry

    lax.fori_loop(0, Y, relayout, 0)

    def far_refs(d):
        sx, sy = neighbours[d]
        px, py = (0 if sx < 0 else X - 1), (0 if sy < 0 else Y - 1)
        if sx and sy:
            return panel.at[:, px, py], lambda e: far_c.at[(0, 1, 2, 3)[(0, 2, 5, 7).index(e)]]
        if sx:
            return panel.at[:, px], lambda e: far_x.at[0 if e == 1 else 1]
        return panel.at[:, :, py], lambda e: far_y.at[0 if e == 3 else 1]

    def far_copy(d, landing):
        source, slot = far_refs(d)
        return pltpu.make_async_remote_copy(
            src_ref=source,
            dst_ref=slot(landing),
            send_sem=far_send.at[d],
            recv_sem=far_recv.at[landing],
            device_id=peer(d),
            device_id_type=MESH,
        )

    for d in range(8):

        @pl.when(exists(d))
        def _():
            far_copy(d, 7 - d).start()

    def diagonal(t, carry):
        first = pl.multiple_of(t * 8, 8)
        v = [panel[c, :, :, pl.ds(first, 8), :] for c in range(3)]
        scale = (27.0 + s_ref[...])[:, :, None, :]
        total = jnp.zeros_like(v[0])
        for c in range(3):
            across = v[c] + shift_lead(v[c], 1, 0) + shift_lead(v[c], -1, 0)
            across = across + shift_lead(across, 1, 1) + shift_lead(across, -1, 1)
            total = total + v[c] * (scale * v[c] - across) - 2.0 * shift_z(v[c], 1) * across
        dz2 = shift_z(v[2], 1) - shift_z(v[2], -1)
        dy1 = shift_lead(v[1], 1, 1) - shift_lead(v[1], -1, 1)
        both = dy1 + dz2
        dx = shift_lead(both, 1, 0) - shift_lead(both, -1, 0)
        dy = shift_lead(dz2, 1, 1) - shift_lead(dz2, -1, 1)
        total = total + 2.0 * mixing * (v[0] * dx + v[1] * dy)
        part = jnp.sum(total.reshape(X * Y, 8, Z), axis=0)
        whole = jnp.sum(part, axis=1, keepdims=True)
        weight[pl.ds(first, 8), :] = jnp.broadcast_to(damping / whole, (8, Z))
        return carry

    lax.fori_loop(0, K // 8, diagonal, 0)

    def restrict(field):
        def body(y, acc):
            for c in range(3):
                for x in range(X):
                    acc = acc + panel[c, x, y] * field[c, x, pl.ds(y, 1), :]
            return acc

        acc = lax.fori_loop(0, Y, body, jnp.zeros((K, Z), jnp.float32))
        return jnp.broadcast_to(jnp.sum(acc, axis=1, keepdims=True), (K, Z))

    def prolong(vector):
        coarse[...] = vector

        def body(k, acc):
            block = z_ref[pl.ds(pl.multiple_of(k * rows, 8), rows), :].reshape(3 * X, Y, Z)
            return acc + block * coarse[pl.ds(k, 1), :][None]

        acc = lax.fori_loop(0, K, body, jnp.zeros((3 * X, Y, Z), jnp.float32), unroll=4)
        return acc.reshape(3, X, Y, Z)

    def put_own(target, field):
        for c in range(3):
            target[c, 2 : X + 2, 0:Y, :] = field[c]

    def operate(field):
        out = stencil(ext, 2, X)
        scale = 27.0 + s_ref[...]
        return [scale * field[c] + out[c][:, 0:Y] for c in range(3)]

    def precondition(turn, current, result):
        first = weight[...] * restrict(current)
        own_p[...] = prolong(first)
        pack_own(turn + 1, own_p)
        launch(turn + 1)
        await_all(turn)
        put_own(ext_r, current)
        unpack_halo(turn, ext_r)
        if turn == 0:
            wide = X + 2
            ext_inv[1 : X + 3] = jnp.zeros((wide, 16, Z), jnp.float32)
            ext_inv[2 : X + 2, 0:Y, :] = s_ref[...]
            for d, (sx, sy) in enumerate(neighbours):
                px, py = (1 if sx < 0 else X + 2), (15 if sy < 0 else 8)
                if sx and sy:
                    ext_inv[px, py, :] = recv[0, d, 3, :]
                elif sx:
                    ext_inv[px, 0:Y] = recv[0, d, 3 * Y : 4 * Y, :]
                else:
                    for x in range(X):
                        ext_inv[2 + x, py, :] = recv[0, d, 3 * X + x, :]
            row = lax.broadcasted_iota(jnp.int32, (wide, 16, Z), 1)
            inside = jnp.logical_or(row <= 8, row == 15)
            ext_inv[1 : X + 3] = jnp.where(inside, damping / (26.0 + ext_inv[1 : X + 3]), 0.0)
        inv = ext_inv[1 : X + 3]
        for c in range(3):
            ext[c, 1 : X + 3] = inv * ext_r[c, 1 : X + 3]
        for _ in range(SWEEPS - 1):
            out = stencil(ext, 1, X + 2)
            new = [
                (1.0 - damping) * ext[c, 1 : X + 3] + inv * (ext_r[c, 1 : X + 3] - ext[c, 1 : X + 3] - out[c])
                for c in range(3)
            ]
            for c in range(3):
                ext[c, 1 : X + 3] = new[c]
        pack_ring(turn + 2)
        launch(turn + 2)
        for c in range(3):
            result[c] = ext[c, 2 : X + 2, 0:Y]
        await_all(turn + 1)
        put_own(ext, own_p)
        unpack_halo(turn + 1, ext)
        image = operate(own_p)
        for c in range(3):
            own_u[c] = current[c] - image[c]
        result[...] += prolong(first + weight[...] * restrict(own_u))
        await_all(turn + 2)
        add_ring(turn + 2, result)

    def image_of(turn, field, result):
        pack_own(turn, field)
        launch(turn)
        put_own(ext, field)
        await_all(turn)
        unpack_halo(turn, ext)
        out = operate(field)
        for c in range(3):
            result[c] = out[c]

    precondition(0, r_ref, own_z)
    image_of(3, own_z, own_w)
    pack_own(4, own_w)
    launch(4)
    precondition(4, own_w, own_v)
    image_of(7, own_v, own_u)

    pairs = ((r_ref, own_z), (own_z, own_w), (r_ref, own_v), (own_w, own_v), (own_z, own_u), (own_v, own_u))
    for i, (a, b) in enumerate(pairs):
        part = jnp.sum((a[...] * b[...]).reshape(3 * X, Y, Z), axis=0)
        dots[i : i + 1, :] = jnp.sum(part, axis=0, keepdims=True)

    def exchange(axis_pos, me, size, buffer, s_sem, r_sem):
        def target(o):
            other = lax.rem(me + o, size)
            return (other, (other, gy) if axis_pos == 0 else (gx, other))

        def copy(o, slot):
            other, where = target(o)
            return pltpu.make_async_remote_copy(
                src_ref=dots,
                dst_ref=buffer.at[me if slot is None else other],
                send_sem=s_sem.at[o],
                recv_sem=r_sem.at[me if slot is None else other],
                device_id=where,
                device_id_type=MESH,
            )

        for o in range(1, size):
            copy(o, None).start()
        buffer[me] = dots[...]
        for o in range(1, size):
            copy(o, 1).wait_recv()
        for o in range(1, size):
            copy(o, None).wait_send()
        dots[...] = jnp.sum(buffer[...], axis=0)

    exchange(0, gx, n_gx, sums_x, sx_send, sx_recv)
    exchange(1, gy, n_gy, sums_y, sy_send, sy_recv)
    total = jnp.sum(dots[...], axis=1, keepdims=True)
    rz, zw, rv, wv, zu, vu = (total[i : i + 1, :] for i in range(6))
    step0 = rz / zw
    rz_new = step0 * (step0 * wv - rv)
    grow = 1.0 + rz_new / rz
    step1 = rz_new / (grow * grow * zw - grow * step0 * (wv + zu) + step0 * step0 * vu)
    keep = jnp.broadcast_to(step0 + step1 * grow, (Y, Z))[None, None]
    cross = jnp.broadcast_to(step1 * step0, (Y, Z))[None, None]
    x_out[...] = keep * own_z[...] - cross * own_v[...]
    res_out[...] = r_ref[...] - keep * own_w[...] + cross * own_u[...]

    for d, (sx, sy) in enumerate(neighbours):
        cells = 1 if sx and sy else (Y if sx else X)

        @pl.when(exists(d))
        def _():
            source, slot = far_refs(d)
            far_copy(d, d).wait_recv()
            other = slot(d)
            if sx and sy:
                parts = ring_image([source[c].reshape(1, K, Z) for c in range(3)], sx, sy)
            else:
                parts = ring_image([source[c] for c in range(3)], sx, sy)
            for c in range(3):
                image_x[c, 0:cells] = parts[c]

            def body(i, acc):
                for c in range(3):
                    right = other[c] if sx and sy else other[c, i]
                    acc = acc + lax.dot_general(
                        split_rows(image_x[c, i]), split_rows(right), (((1,), (1,)), ((), ())),
                        preferred_element_type=jnp.float32,
                    )
                return acc

            acc = lax.fori_loop(0, cells, body, jnp.zeros((2 * K, 2 * K), jnp.float32))
            half = acc[0:K] + acc[K : 2 * K]
            tile_out[d] = half[:, 0:K] + half[:, K : 2 * K]

        @pl.when(jnp.logical_not(exists(d)))
        def _():
            tile_out[d] = jnp.zeros((K, K), jnp.float32)

    for d in range(8):

        @pl.when(exists(d))
        def _():
            far_copy(d, 7 - d).wait_send()
            for turn in range(ROUNDS):
                message(turn, d).wait_send()


def per_device(n_gx, n_gy, right_side, stiffness, panels):
    X, Y, Z = stiffness.shape
    K = panels.shape[0]
    f32 = jnp.float32
    field = pltpu.VMEM((3, X, Y, Z), f32)
    dma = pltpu.SemaphoreType.DMA
    vmem = pl.BlockSpec(memory_space=pltpu.VMEM)
    x, res, tiles = pl.pallas_call(
        functools.partial(kernel, n_gx, n_gy),
        out_shape=(
            jax.ShapeDtypeStruct((3, X, Y, Z), f32),
            jax.ShapeDtypeStruct((3, X, Y, Z), f32),
            jax.ShapeDtypeStruct((8, K, K), f32),
        ),
        in_specs=[vmem] * 3,
        out_specs=(vmem,) * 3,
        scratch_shapes=[
            pltpu.VMEM((3, X, Y, K, Z), f32),
            pltpu.VMEM((2, 3, Y, K, Z), f32),
            pltpu.VMEM((2, 3, X, K, Z), f32),
            pltpu.VMEM((4, 3, K, Z), f32),
            pltpu.VMEM((3, Y, K, Z), f32),
            pltpu.VMEM((ROUNDS, 8, 32, Z), f32),
            pltpu.VMEM((ROUNDS, 8, 32, Z), f32),
            pltpu.VMEM((3, X + 4, 16, Z), f32),
            pltpu.VMEM((3, X + 4, 16, Z), f32),
            pltpu.VMEM((X + 4, 16, Z), f32),
            field, field, field, field, field,
            pltpu.VMEM((K, Z), f32),
            pltpu.VMEM((K, Z), f32),
            pltpu.VMEM((8, Z), f32),
            pltpu.VMEM((n_gx, 8, Z), f32),
            pltpu.VMEM((n_gy, 8, Z), f32),
            dma((ROUNDS, 8)), dma((ROUNDS, 8)), dma((8,)), dma((8,)),
            dma((n_gx,)), dma((n_gx,)), dma((n_gy,)), dma((n_gy,)),
        ],
        compiler_params=pltpu.CompilerParams(
            collective_id=0, has_side_effects=True, vmem_limit_bytes=48 * 1024 * 1024
        ),
    )(right_side, stiffness, panels.reshape(K * 3 * X * Y, Z))
    return x, res, tiles.reshape(1, 1, 8, K * K)


def solution(mesh):
    n_gx, n_gy = mesh.shape["gx"], mesh.shape["gy"]
    return jax.shard_map(
        functools.partial(per_device, n_gx, n_gy),
        mesh=mesh,
        in_specs=(P(None, "gx", "gy", None), P("gx", "gy", None), P(None, None, "gx", "gy", None)),
        out_specs=(P(None, "gx", "gy", None), P(None, "gx", "gy", None), P("gx", "gy", None, None)),
        check_vma=False,
    )
```

profile of v0, /device:TPU:3, one launch (start us, length us, event | category | flops | bytes accessed | tf_op | source)
XLA Modules:
  0.0 89.5 jit_solution(14000789633467522584)
XLA Ops:
  0.6 0.0 copy-start
  0.6 1.9 %copy-done = f32[64,3,4,8,128]{4,3,2,1,0:T(8,128)S(1)} copy-done((f32[64,3,4,8,128]{4,3,2,1,0:T(8,128)S(1)}, f32[64,3,4,8,128]{4,3,2,1,0:T(8,128)}, u32[]{:S(2)}) %copy-start) | copy-done | bytes 3145752
  2.5 0.0 copy-start.1
  2.5 0.8 copy-done.1
  3.3 0.0 copy-start.2
  3.3 0.7 copy-done.2
  4.0 83.5 %shard_map.58 = (f32[3,4,8,128]{3,2,1,0:T(8,128)S(1)}, f32[3,4,8,128]{3,2,1,0:T(8,128)S(1)}, f32[8,64,64]{2,1,0:T(8,128)S(1)}) custom-call(f32[3,4,8,128]{3,2,1,0:T(8,128)S(1)} %copy-done.1, f32[4,8,128]{2,1,0:T(8,128)S(1)} %copy-done.2, f32[6144,128]{1,0:T(8,128)S(1)} %bitcast.1), custom_call_target="tpu_custom_call" | custom-call | tf_op jit(solution)/shard_map/pallas_call | solution.py:495
  87.5 0.8 reshape.13
  88.3 0.6 copy.8
  88.9 0.6 copy.9
Async XLA Ops:
  0.6 1.9 %copy-start = (f32[64,3,4,8,128]{4,3,2,1,0:T(8,128)S(1)}, f32[64,3,4,8,128]{4,3,2,1,0:T(8,128)}, u32[]{:S(2)}) copy-start(f32[64,3,4,8,128]{4,3,2,1,0:T(8,128)} %param.5) | copy-start | bytes 9437188
  2.5 0.8 copy-start.1
  3.3 0.7 copy-start.2
where the time goes:
time: 89.8 us; the launch traced here: 89.5 us
  Pallas kernels  83.5 us (93%)
  local copies, waits for them, and re-layouts  5.41 us (6%)
    pallas_call x1, Pallas kernels, per_device(): pl.pallas_call(functools.partial(kernel, n_gx, n_gy), out_shape=(jax.Shap...  83.5 us
    unnamed x8, local copies, waits for them, and re-layouts  4.64 us

commit v1 on v0

--- a/solution.py
+++ b/solution.py
@@ -99,10 +99,10 @@
 
 
 def kernel(
-    n_gx, n_gy, r_ref, s_ref, z_ref, x_out, res_out, tile_out,
-    panel, far_x, far_y, far_c, image_x, send, recv, ext, ext_r, ext_inv, own_p, own_z, own_w, own_v, own_u,
+    n_gx, n_gy, r_hbm, s_hbm, z_hbm, x_out, res_out, tile_out,
+    r_ref, s_ref, z_ref, panel, far_x, far_y, far_c, image_x, image_y, image_c, share, share_far, send, recv, ext, ext_r, ext_inv, own_p, own_z, own_w, own_v, own_u,
     weight, coarse, dots, sums_x, sums_y,
-    send_sem, recv_sem, far_send, far_recv, sx_send, sx_recv, sy_send, sy_recv,
+    in_sem, send_sem, recv_sem, far_send, far_recv, part_send, part_recv, sx_send, sx_recv, sy_send, sy_recv,
 ):
     X, Y, Z = s_ref.shape
     K = panel.shape[3]
@@ -124,6 +124,12 @@
     def peer(d):
         return (gx + neighbours[d][0], gy + neighbours[d][1])
 
+    load_z = pltpu.make_async_copy(z_hbm, z_ref, in_sem.at[0])
+    load_r = pltpu.make_async_copy(r_hbm, r_ref, in_sem.at[1])
+    load_s = pltpu.make_async_copy(s_hbm, s_ref, in_sem.at[2])
+    load_r.start()
+    load_s.start()
+    load_z.start()
     recv[...] = jnp.zeros_like(recv)
     ext[...] = jnp.zeros_like(ext)
     ext_r[...] = jnp.zeros_like(ext_r)
@@ -142,6 +148,8 @@
         def _():
             pl.semaphore_signal(barrier, inc=1, device_id=peer(d), device_id_type=MESH)
 
+    load_r.wait()
+    load_s.wait()
     pl.semaphore_wait(barrier, count)
 
     def length(d, with_stiff):
@@ -256,33 +264,110 @@
                     panel[c, x, y, t * 8 : t * 8 + 8, :] = z_ref[pl.ds(row, 8, stride=rows), :]
         return carry
 
+    load_z.wait()
     lax.fori_loop(0, Y, relayout, 0)
 
-    def far_refs(d):
+    hx, hy = X // 2, Y // 2
+
+    def far_copy(d):
+        source, slot = {
+            1: lambda: (panel.at[:, 0, 0:hy], far_x.at[1]),
+            3: lambda: (panel.at[:, 0:hx, 0], far_y.at[1]),
+            0: lambda: (panel.at[:, 0, 0], far_c.at[1]),
+            6: lambda: (image_x.at[:, hy:Y], far_x.at[0]),
+            4: lambda: (image_y.at[:, hx:X], far_y.at[0]),
+            5: lambda: (image_c.at[0], far_c.at[0]),
+        }[d]()
+        return pltpu.make_async_remote_copy(
+            src_ref=source, dst_ref=slot, send_sem=far_send.at[d], recv_sem=far_recv.at[7 - d],
+            device_id=peer(d), device_id_type=MESH,
+        )
+
+    def far_arrival(d):
+        slot = {6: (far_x, 1), 4: (far_y, 1), 7: (far_c, 1), 1: (far_x, 0), 3: (far_y, 0), 2: (far_c, 0)}[d]
+        here = slot[0].at[slot[1]]
+        return pltpu.make_async_remote_copy(
+            src_ref=here, dst_ref=here, send_sem=far_send.at[d], recv_sem=far_recv.at[d],
+            device_id=peer(d), device_id_type=MESH,
+        )
+
+    def far_start(d):
+        @pl.when(exists(d))
+        def _():
+            far_copy(d).start()
+
+    def make_image(d):
         sx, sy = neighbours[d]
         px, py = (0 if sx < 0 else X - 1), (0 if sy < 0 else Y - 1)
-        if sx and sy:
-            return panel.at[:, px, py], lambda e: far_c.at[(0, 1, 2, 3)[(0, 2, 5, 7).index(e)]]
-        if sx:
-            return panel.at[:, px], lambda e: far_x.at[0 if e == 1 else 1]
-        return panel.at[:, :, py], lambda e: far_y.at[0 if e == 3 else 1]
-
-    def far_copy(d, landing):
-        source, slot = far_refs(d)
-        return pltpu.make_async_remote_copy(
-            src_ref=source,
-            dst_ref=slot(landing),
-            send_sem=far_send.at[d],
-            recv_sem=far_recv.at[landing],
-            device_id=peer(d),
-            device_id_type=MESH,
-        )
-
-    for d in range(8):
 
         @pl.when(exists(d))
         def _():
-            far_copy(d, 7 - d).start()
+            if sx and sy:
+                parts = ring_image([panel[c, px, py].reshape(1, K, Z) for c in range(3)], sx, sy)
+                for c in range(3):
+                    image_c[0 if d == 5 else 1, c] = parts[c].reshape(K, Z)
+            elif sx:
+                parts = ring_image([panel[c, px] for c in range(3)], sx, sy)
+                for c in range(3):
+                    image_x[c] = parts[c]
+            else:
+                parts = ring_image([panel[c, :, py] for c in range(3)], sx, sy)
+                for c in range(3):
+                    image_y[c] = parts[c]
+
+    def part_copy(d):
+        return pltpu.make_async_remote_copy(
+            src_ref=share.at[d], dst_ref=share_far.at[7 - d], send_sem=part_send.at[d], recv_sem=part_recv.at[7 - d],
+            device_id=peer(d), device_id_type=MESH,
+        )
+
+    def part_arrival(d):
+        return pltpu.make_async_remote_copy(
+            src_ref=share.at[d], dst_ref=share_far.at[d], send_sem=part_send.at[d], recv_sem=part_recv.at[d],
+            device_id=peer(d), device_id_type=MESH,
+        )
+
+    def make_part(d):
+        @pl.when(exists(d))
+        def _():
+            far_arrival(d).wait_recv()
+            left, right = [], []
+            for c in range(3):
+                if d == 6:
+                    for y in range(hy):
+                        left.append(image_x[c, y])
+                        right.append(far_x[1, c, y])
+                elif d == 4:
+                    for x in range(hx):
+                        left.append(image_y[c, x])
+                        right.append(far_y[1, c, x])
+                elif d == 7:
+                    left.append(image_c[1, c])
+                    right.append(far_c[1, c])
+                elif d == 1:
+                    for y in range(hy, Y):
+                        left.append(far_x[0, c, y - hy])
+                        right.append(panel[c, 0, y])
+                elif d == 3:
+                    for x in range(hx, X):
+                        left.append(far_y[0, c, x - hx])
+                        right.append(panel[c, x, 0])
+                else:
+                    left.append(far_c[0, c])
+                    right.append(panel[c, 0, Y - 1])
+            acc = lax.dot_general(
+                jnp.concatenate([split_rows(v) for v in left], axis=1),
+                jnp.concatenate([split_rows(v) for v in right], axis=1),
+                (((1,), (1,)), ((), ())),
+                preferred_element_type=jnp.float32,
+            )
+            half = acc[0:K] + acc[K : 2 * K]
+            tile = half[:, 0:K] + half[:, K : 2 * K]
+            share[d] = jnp.concatenate([tile[0 : K // 2], tile[K // 2 : K]], axis=1)
+            part_copy(d).start()
+
+    for d in (1, 3, 0):
+        far_start(d)
 
     def diagonal(t, carry):
         first = pl.multiple_of(t * 8, 8)
@@ -372,6 +457,12 @@
                 ext[c, 1 : X + 3] = new[c]
         pack_ring(turn + 2)
         launch(turn + 2)
+        if turn == 0:
+            make_image(6)
+            far_start(6)
+        else:
+            for d in (1, 2, 3):
+                make_part(d)
         for c in range(3):
             result[c] = ext[c, 2 : X + 2, 0:Y]
         await_all(turn + 1)
@@ -388,6 +479,12 @@
         pack_own(turn, field)
         launch(turn)
         put_own(ext, field)
+        if turn == 3:
+            make_image(4)
+            far_start(4)
+            make_image(5)
+            far_start(5)
+            make_image(7)
         await_all(turn)
         unpack_halo(turn, ext)
         out = operate(field)
@@ -398,6 +495,8 @@
     image_of(3, own_z, own_w)
     pack_own(4, own_w)
     launch(4)
+    for d in (6, 4, 7):
+        make_part(d)
     precondition(4, own_w, own_v)
     image_of(7, own_v, own_u)
 
@@ -444,33 +543,16 @@
     x_out[...] = keep * own_z[...] - cross * own_v[...]
     res_out[...] = r_ref[...] - keep * own_w[...] + cross * own_u[...]
 
-    for d, (sx, sy) in enumerate(neighbours):
-        cells = 1 if sx and sy else (Y if sx else X)
+    for d in range(8):
 
         @pl.when(exists(d))
         def _():
-            source, slot = far_refs(d)
-            far_copy(d, d).wait_recv()
-            other = slot(d)
-            if sx and sy:
-                parts = ring_image([source[c].reshape(1, K, Z) for c in range(3)], sx, sy)
-            else:
-                parts = ring_image([source[c] for c in range(3)], sx, sy)
-            for c in range(3):
-                image_x[c, 0:cells] = parts[c]
-
-            def body(i, acc):
-                for c in range(3):
-                    right = other[c] if sx and sy else other[c, i]
-                    acc = acc + lax.dot_general(
-                        split_rows(image_x[c, i]), split_rows(right), (((1,), (1,)), ((), ())),
-                        preferred_element_type=jnp.float32,
-                    )
-                return acc
-
-            acc = lax.fori_loop(0, cells, body, jnp.zeros((2 * K, 2 * K), jnp.float32))
-            half = acc[0:K] + acc[K : 2 * K]
-            tile_out[d] = half[:, 0:K] + half[:, K : 2 * K]
+            whole = share[d] if d in (2, 7) else None
+            if d not in (2, 7):
+                part_arrival(d).wait_recv()
+                whole = share_far[d] if d in (0, 5) else share[d] + share_far[d]
+            tile = jnp.concatenate([whole[:, 0:K], whole[:, K : 2 * K]], axis=0)
+            tile_out[d] = tile if d >= 4 else tile.T
 
         @pl.when(jnp.logical_not(exists(d)))
         def _():
@@ -480,7 +562,10 @@
 
         @pl.when(exists(d))
         def _():
-            far_copy(d, 7 - d).wait_send()
+            if d not in (2, 7):
+                far_copy(d).wait_send()
+            if d not in (0, 5):
+                part_copy(d).wait_send()
             for turn in range(ROUNDS):
                 message(turn, d).wait_send()
 
@@ -499,14 +584,21 @@
             jax.ShapeDtypeStruct((3, X, Y, Z), f32),
             jax.ShapeDtypeStruct((8, K, K), f32),
         ),
-        in_specs=[vmem] * 3,
+        in_specs=[pl.BlockSpec(memory_space=pl.ANY)] * 3,
         out_specs=(vmem,) * 3,
         scratch_shapes=[
+            field,
+            pltpu.VMEM((X, Y, Z), f32),
+            pltpu.VMEM((K * 3 * X * Y, Z), f32),
             pltpu.VMEM((3, X, Y, K, Z), f32),
-            pltpu.VMEM((2, 3, Y, K, Z), f32),
-            pltpu.VMEM((2, 3, X, K, Z), f32),
-            pltpu.VMEM((4, 3, K, Z), f32),
+            pltpu.VMEM((2, 3, Y // 2, K, Z), f32),
+            pltpu.VMEM((2, 3, X // 2, K, Z), f32),
+            pltpu.VMEM((2, 3, K, Z), f32),
             pltpu.VMEM((3, Y, K, Z), f32),
+            pltpu.VMEM((3, X, K, Z), f32),
+            pltpu.VMEM((2, 3, K, Z), f32),
+            pltpu.VMEM((8, K // 2, 2 * K), f32),
+            pltpu.VMEM((8, K // 2, 2 * K), f32),
             pltpu.VMEM((ROUNDS, 8, 32, Z), f32),
             pltpu.VMEM((ROUNDS, 8, 32, Z), f32),
             pltpu.VMEM((3, X + 4, 16, Z), f32),
@@ -518,11 +610,11 @@
             pltpu.VMEM((8, Z), f32),
             pltpu.VMEM((n_gx, 8, Z), f32),
             pltpu.VMEM((n_gy, 8, Z), f32),
-            dma((ROUNDS, 8)), dma((ROUNDS, 8)), dma((8,)), dma((8,)),
+            dma((3,)), dma((ROUNDS, 8)), dma((ROUNDS, 8)), dma((8,)), dma((8,)), dma((8,)), dma((8,)),
             dma((n_gx,)), dma((n_gx,)), dma((n_gy,)), dma((n_gy,)),
         ],
         compiler_params=pltpu.CompilerParams(
-            collective_id=0, has_side_effects=True, vmem_limit_bytes=48 * 1024 * 1024
+            collective_id=0, has_side_effects=True, vmem_limit_bytes=56 * 1024 * 1024
         ),
     )(right_side, stiffness, panels.reshape(K * 3 * X * Y, Z))
     return x, res, tiles.reshape(1, 1, 8, K * K)

time: 89.8 us -> 57.6 us (0.64)
  Pallas kernels: 83.5 us -> 51.5 us
    pallas_call x1, Pallas kernels: 83.5 us -> 51.5 us  [per_device(): pl.pallas_call(functools.partial(kernel, n_gx, n_gy), out_shape=(jax.Shap...]
    unnamed x8 -> x2, local copies, waits for them, and re-layouts: 4.64 us -> 2.84 us
    reshape x1, local copies, waits for them, and re-layouts: 0.77 us -> 1.72 us  [per_device(): return (x, res, tiles.reshape(1, 1, 8, K * K))]
where the time goes in v1:
time: 57.6 us; the launch traced here: 56.7 us
  Pallas kernels  51.5 us (89%)
  local copies, waits for them, and re-layouts  4.56 us (8%)
  between operations  0.64 us (1%)
    pallas_call x1, Pallas kernels, per_device(): pl.pallas_call(functools.partial(kernel, n_gx, n_gy), out_shape=(jax.Shap...  51.5 us
    unnamed x2, local copies, waits for them, and re-layouts  2.84 us
    reshape x1, local copies, waits for them, and re-layouts, per_device(): return (x, res, tiles.reshape(1, 1, 8, K * K))  1.72 us

profile of v1, /device:TPU:3, one launch (start us, length us, event | category | flops | bytes accessed | tf_op | source)
XLA Modules:
  0.0 56.7 jit_solution(8315268761924947036)
XLA Ops:
  0.6 51.5 %shard_map.58 = (f32[3,4,8,128]{3,2,1,0:T(8,128)}, f32[3,4,8,128]{3,2,1,0:T(8,128)}, f32[8,64,64]{2,1,0:T(8,128)}) custom-call(f32[3,4,8,128]{3,2,1,0:T(8,128)} %r_hbm.1, f32[4,8,128]{2,1,0:T(8,128)} %s_hbm.1, f32[6144,128]{1,0:T(8,128)} %bitcast.1), custom_call_target="tpu_custom_call" | custom-call | tf_op jit(solution)/shard_map/pallas_call | solution.py:580
  52.2 1.7 %reshape.13 = f32[1,1,8,4096]{3,2,1,0:T(8,128)} reshape(f32[8,64,64]{2,1,0:T(8,128)} %get-tuple-element.8) | data formatting | bytes 262144 | tf_op jit(solution)/shard_map/reshape | solution.py:620
  53.9 1.4 %copy.8 = f32[3,4,8,128]{3,2,1,0:T(8,128)} copy(f32[3,4,8,128]{3,2,1,0:T(8,128)} %get-tuple-element.12) | data formatting | bytes 98304
  55.3 1.4 %copy.9 = f32[3,4,8,128]{3,2,1,0:T(8,128)} copy(f32[3,4,8,128]{3,2,1,0:T(8,128)} %get-tuple-element.13) | data formatting | bytes 98304

commit v2 on v1

--- a/solution.py
+++ b/solution.py
@@ -12,7 +12,8 @@
 mixing = 0.25
 damping = 0.5
 neighbours = ((-1, -1), (-1, 0), (-1, 1), (0, -1), (0, 1), (1, -1), (1, 0), (1, 1))
-ROUNDS = 8
+ROUNDS = 6
+STRIPS = (2, 5)
 
 
 def shift_z(value, step):
@@ -32,9 +33,10 @@
     return jnp.concatenate([zero, lax.slice_in_dim(value, 0, size - 1, axis=axis)], axis=axis)
 
 
-def stencil(field, start, count):
+def stencil(field, wide, start, count):
     def planes(c, step):
-        return field[c, start + step : start + step + count]
+        first = (c * wide + start + step) * 16
+        return field[first : first + count * 16, :].reshape(count, 16, field.shape[1])
 
     def up(v):
         return pltpu.roll(v, 15, 1)
@@ -100,12 +102,12 @@
 
 def kernel(
     n_gx, n_gy, r_hbm, s_hbm, z_hbm, x_out, res_out, tile_out,
-    r_ref, s_ref, z_ref, panel, far_x, far_y, far_c, image_x, image_y, image_c, share, share_far, send, recv, ext, ext_r, ext_inv, own_p, own_z, own_w, own_v, own_u,
-    weight, coarse, dots, sums_x, sums_y,
+    r_ref, s_ref, z_ref, panel, far_x, far_y, far_c, image_x, image_y, image_c, share, share_far, send, recv, ext, ext_r, ext_p, ext_inv, own_p, own_z, own_w, own_v, own_u,
+    weight, coarse, square, packed, dots, sums_x, sums_y,
     in_sem, send_sem, recv_sem, far_send, far_recv, part_send, part_recv, sx_send, sx_recv, sy_send, sy_recv,
 ):
-    X, Y, Z = s_ref.shape
-    K = panel.shape[3]
+    X, Y, K, Z = panel.shape[1:]
+    wide = X + 4
     rows = 3 * X * Y
     gx, gy = lax.axis_index("gx"), lax.axis_index("gy")
 
@@ -133,6 +135,7 @@
     recv[...] = jnp.zeros_like(recv)
     ext[...] = jnp.zeros_like(ext)
     ext_r[...] = jnp.zeros_like(ext_r)
+    ext_p[...] = jnp.zeros_like(ext_p)
     ext_inv[...] = jnp.zeros_like(ext_inv)
     dots[...] = jnp.zeros_like(dots)
     barrier = pltpu.get_barrier_semaphore()
@@ -150,18 +153,32 @@
 
     load_r.wait()
     load_s.wait()
+
+    def relayout(y, carry):
+        for c in range(3):
+            for x in range(X):
+                for t in range(K // 8):
+                    row = (c * X + x) * Y + y + t * 8 * rows
+                    panel[c, x, y, t * 8 : t * 8 + 8, :] = z_ref[pl.ds(row, 8, stride=rows), :]
+        return carry
+
+    load_z.wait()
+    lax.fori_loop(0, Y, relayout, 0)
+
     pl.semaphore_wait(barrier, count)
 
-    def length(d, with_stiff):
+    def length(turn, d):
         sx, sy = neighbours[d]
+        if turn in STRIPS:
+            return 16 if sx and sy else (64 if sx else 48)
         if sx and sy:
             return 8
         if sx:
-            return 32 if with_stiff else 24
+            return 32 if turn == 0 else 24
         return 16
 
     def message(turn, d):
-        n = length(d, turn == 0)
+        n = length(turn, d)
         return pltpu.make_async_remote_copy(
             src_ref=send.at[turn, d, 0:n],
             dst_ref=recv.at[turn, 7 - d, 0:n],
@@ -172,7 +189,7 @@
         )
 
     def arrival(turn, d):
-        n = length(d, turn == 0)
+        n = length(turn, d)
         return pltpu.make_async_remote_copy(
             src_ref=send.at[turn, d, 0:n],
             dst_ref=recv.at[turn, d, 0:n],
@@ -199,73 +216,88 @@
     def pack_own(turn, field):
         for d, (sx, sy) in enumerate(neighbours):
             px, py = (0 if sx < 0 else X - 1), (0 if sy < 0 else Y - 1)
+            if sx and sy:
+                send[turn, d, 0:3, :] = field[pl.ds(px * Y + py, 3, stride=X * Y), :]
+                continue
             for c in range(3):
-                if sx and sy:
-                    send[turn, d, c, :] = field[c, px, py, :]
-                elif sx:
-                    send[turn, d, c * Y : (c + 1) * Y, :] = field[c, px]
+                if sx:
+                    first = (c * X + px) * Y
+                    send[turn, d, c * Y : (c + 1) * Y, :] = field[first : first + Y, :]
                 else:
-                    for x in range(X):
-                        send[turn, d, c * X + x, :] = field[c, x, py, :]
-
-    def pack_ring(turn):
-        for d, (sx, sy) in enumerate(neighbours):
-            px, py = (1 if sx < 0 else X + 2), (15 if sy < 0 else 8)
-            for c in range(3):
-                if sx and sy:
-                    send[turn, d, c, :] = ext[c, px, py, :]
-                elif sx:
-                    send[turn, d, c * Y : (c + 1) * Y, :] = ext[c, px, 0:Y]
-                else:
-                    for x in range(X):
-                        send[turn, d, c * X + x, :] = ext[c, 2 + x, py, :]
+                    send[turn, d, c * X : (c + 1) * X, :] = field[pl.ds(c * X * Y + py, X, stride=Y), :]
 
     def unpack_halo(turn, target):
         for d, (sx, sy) in enumerate(neighbours):
             px, py = (1 if sx < 0 else X + 2), (15 if sy < 0 else 8)
+            if sx and sy:
+                target[pl.ds(px * 16 + py, 3, stride=wide * 16), :] = recv[turn, d, 0:3, :]
+                continue
             for c in range(3):
-                if sx and sy:
-                    target[c, px, py, :] = recv[turn, d, c, :]
-                elif sx:
-                    target[c, px, 0:Y] = recv[turn, d, c * Y : (c + 1) * Y, :]
+                if sx:
+                    first = (c * wide + px) * 16
+                    target[first : first + Y, :] = recv[turn, d, c * Y : (c + 1) * Y, :]
                 else:
-                    for x in range(X):
-                        target[c, 2 + x, py, :] = recv[turn, d, c * X + x, :]
-
-    def add_ring(turn, target):
+                    first = (c * wide + 2) * 16 + py
+                    target[pl.ds(first, X, stride=16), :] = recv[turn, d, c * X : (c + 1) * X, :]
+
+    def strips(turn, visit):
         for d, (sx, sy) in enumerate(neighbours):
-            px, py = (0 if sx < 0 else X - 1), (0 if sy < 0 else Y - 1)
-            for c in range(3):
-                if sx and sy:
-                    target[c, px, py, :] += recv[turn, d, c, :]
-                elif sx:
-                    target[c, px] += recv[turn, d, c * Y : (c + 1) * Y, :]
-                else:
-                    for x in range(X):
-                        target[c, x, py, :] += recv[turn, d, c * X + x, :]
+            p0, ys = (1 if sx < 0 else X + 1), ((15, 0) if sy < 0 else (7, 8))
+            if sx == 0:
+                for c in range(3):
+                    for t in range(2):
+                        first = (c * 2 + t) * 8
+                        visit(d, pl.ds((c * wide + 1) * 16 + ys[t], X + 2, stride=16), slice(first, first + X + 2))
+                continue
+            if sy == 0:
+                for c in range(3):
+                    for p in range(2):
+                        first, row = (c * 2 + p) * 8, (c * wide + p0 + p) * 16
+                        visit(d, slice(row, row + 8), slice(first, first + 8))
+                ys = (15, 8)
+            base = 48 if sy == 0 else 0
+            for p in range(2):
+                for t in range(2):
+                    first = base + (p * 2 + t) * 4
+                    visit(d, pl.ds((p0 + p) * 16 + ys[t], 3, stride=wide * 16), slice(first, first + 3))
+
+    def pack_strips(turn):
+        def visit(d, here, there):
+            send[turn, d, there, :] = ext[here, :]
+
+        strips(turn, visit)
+
+    def add_strips(turn):
+        def visit(d, here, there):
+            ext[here, :] = ext[here, :] + recv[turn, d, there, :]
+
+        strips(turn, visit)
+        for ok, plane in ((gx == 0, 1), (gx == n_gx - 1, X + 2)):
+
+            @pl.when(ok)
+            def _():
+                for c in range(3):
+                    first = (c * wide + plane) * 16
+                    ext[first : first + 16, :] = jnp.zeros((16, Z), jnp.float32)
+
+        for ok, row in ((gy == 0, 15), (gy == n_gy - 1, 8)):
+
+            @pl.when(ok)
+            def _():
+                for c in range(3):
+                    first = (c * wide + 1) * 16 + row
+                    ext[pl.ds(first, X + 2, stride=16), :] = jnp.zeros((X + 2, Z), jnp.float32)
 
     pack_own(0, r_ref)
     for d, (sx, sy) in enumerate(neighbours):
         px, py = (0 if sx < 0 else X - 1), (0 if sy < 0 else Y - 1)
         if sx and sy:
-            send[0, d, 3, :] = s_ref[px, py, :]
+            send[0, d, 3:4, :] = s_ref[px * Y + py : px * Y + py + 1, :]
         elif sx:
-            send[0, d, 3 * Y : 4 * Y, :] = s_ref[px]
+            send[0, d, 3 * Y : 4 * Y, :] = s_ref[px * Y : (px + 1) * Y, :]
         else:
-            for x in range(X):
-                send[0, d, 3 * X + x, :] = s_ref[x, py, :]
+            send[0, d, 3 * X : 4 * X, :] = s_ref[pl.ds(py, X, stride=Y), :]
     launch(0)
-
-    def relayout(y, carry):
-        for c in range(3):
-            for x in range(X):
-                for t in range(K // 8):
-                    row = (c * X + x) * Y + y + t * 8 * rows
-                    panel[c, x, y, t * 8 : t * 8 + 8, :] = z_ref[pl.ds(row, 8, stride=rows), :]
-        return carry
-
-    load_z.wait()
-    lax.fori_loop(0, Y, relayout, 0)
 
     hx, hy = X // 2, Y // 2
 
@@ -372,7 +404,7 @@
     def diagonal(t, carry):
         first = pl.multiple_of(t * 8, 8)
         v = [panel[c, :, :, pl.ds(first, 8), :] for c in range(3)]
-        scale = (27.0 + s_ref[...])[:, :, None, :]
+        scale = (27.0 + s_ref[...].reshape(X, Y, Z))[:, :, None, :]
         total = jnp.zeros_like(v[0])
         for c in range(3):
             across = v[c] + shift_lead(v[c], 1, 0) + shift_lead(v[c], -1, 0)
@@ -395,7 +427,7 @@
         def body(y, acc):
             for c in range(3):
                 for x in range(X):
-                    acc = acc + panel[c, x, y] * field[c, x, pl.ds(y, 1), :]
+                    acc = acc + panel[c, x, y] * field[pl.ds((c * X + x) * Y + y, 1), :]
             return acc
 
         acc = lax.fori_loop(0, Y, body, jnp.zeros((K, Z), jnp.float32))
@@ -409,103 +441,106 @@
             return acc + block * coarse[pl.ds(k, 1), :][None]
 
         acc = lax.fori_loop(0, K, body, jnp.zeros((3 * X, Y, Z), jnp.float32), unroll=4)
-        return acc.reshape(3, X, Y, Z)
+        return acc.reshape(rows, Z)
 
     def put_own(target, field):
         for c in range(3):
-            target[c, 2 : X + 2, 0:Y, :] = field[c]
-
-    def operate(field):
-        out = stencil(ext, 2, X)
+            for x in range(X):
+                here, there = (c * wide + 2 + x) * 16, (c * X + x) * Y
+                target[here : here + Y, :] = field[there : there + Y, :]
+
+    def operate(padded, field):
+        out = stencil(padded, wide, 2, X)
         scale = 27.0 + s_ref[...]
-        return [scale * field[c] + out[c][:, 0:Y] for c in range(3)]
-
-    def precondition(turn, current, result):
+        per = X * Y
+        return [scale * field[c * per : (c + 1) * per, :] + out[c][:, 0:Y].reshape(per, Z) for c in range(3)]
+
+    def inner(ref, c):
+        first = (c * wide + 1) * 16
+        return slice(first, first + (X + 2) * 16)
+
+    def apply_both(turn, current, result, image, filler):
         first = weight[...] * restrict(current)
         own_p[...] = prolong(first)
         pack_own(turn + 1, own_p)
         launch(turn + 1)
+        put_own(ext_r, current)
+        put_own(ext_p, own_p)
         await_all(turn)
-        put_own(ext_r, current)
         unpack_halo(turn, ext_r)
         if turn == 0:
-            wide = X + 2
-            ext_inv[1 : X + 3] = jnp.zeros((wide, 16, Z), jnp.float32)
-            ext_inv[2 : X + 2, 0:Y, :] = s_ref[...]
+            for x in range(X):
+                ext_inv[(2 + x) * 16 : (2 + x) * 16 + Y, :] = s_ref[x * Y : (x + 1) * Y, :]
             for d, (sx, sy) in enumerate(neighbours):
                 px, py = (1 if sx < 0 else X + 2), (15 if sy < 0 else 8)
                 if sx and sy:
-                    ext_inv[px, py, :] = recv[0, d, 3, :]
+                    ext_inv[px * 16 + py : px * 16 + py + 1, :] = recv[0, d, 3:4, :]
                 elif sx:
-                    ext_inv[px, 0:Y] = recv[0, d, 3 * Y : 4 * Y, :]
+                    ext_inv[px * 16 : px * 16 + Y, :] = recv[0, d, 3 * Y : 4 * Y, :]
                 else:
-                    for x in range(X):
-                        ext_inv[2 + x, py, :] = recv[0, d, 3 * X + x, :]
-            row = lax.broadcasted_iota(jnp.int32, (wide, 16, Z), 1)
+                    ext_inv[pl.ds(2 * 16 + py, X, stride=16), :] = recv[0, d, 3 * X : 4 * X, :]
+            shape = ((X + 2) * 16, Z)
+            row = lax.rem(lax.broadcasted_iota(jnp.int32, shape, 0), 16)
             inside = jnp.logical_or(row <= 8, row == 15)
-            ext_inv[1 : X + 3] = jnp.where(inside, damping / (26.0 + ext_inv[1 : X + 3]), 0.0)
-        inv = ext_inv[1 : X + 3]
+            stiff = ext_inv[16 : (X + 3) * 16, :]
+            ext_inv[16 : (X + 3) * 16, :] = jnp.where(inside, damping / (26.0 + stiff), 0.0)
+        inv = ext_inv[16 : (X + 3) * 16, :]
         for c in range(3):
-            ext[c, 1 : X + 3] = inv * ext_r[c, 1 : X + 3]
+            ext[inner(ext, c), :] = inv * ext_r[inner(ext, c), :]
         for _ in range(SWEEPS - 1):
-            out = stencil(ext, 1, X + 2)
-            new = [
-                (1.0 - damping) * ext[c, 1 : X + 3] + inv * (ext_r[c, 1 : X + 3] - ext[c, 1 : X + 3] - out[c])
-                for c in range(3)
-            ]
+            out = stencil(ext, wide, 1, X + 2)
+            new = []
             for c in range(3):
-                ext[c, 1 : X + 3] = new[c]
-        pack_ring(turn + 2)
+                e = ext[inner(ext, c), :]
+                change = ext_r[inner(ext, c), :] - e - out[c].reshape((X + 2) * 16, Z)
+                new.append((1.0 - damping) * e + inv * change)
+            for c in range(3):
+                ext[inner(ext, c), :] = new[c]
+        await_all(turn + 1)
+        unpack_halo(turn + 1, ext_p)
+        coarse_image = operate(ext_p, own_p)
+        per = X * Y
+        for c in range(3):
+            own_u[c * per : (c + 1) * per, :] = current[c * per : (c + 1) * per, :] - coarse_image[c]
+        own_p[...] = prolong(first + weight[...] * restrict(own_u))
+        for c in range(3):
+            for x in range(X):
+                here, there = (c * wide + 2 + x) * 16, (c * X + x) * Y
+                ext[here : here + Y, :] = ext[here : here + Y, :] + own_p[there : there + Y, :]
+        pack_strips(turn + 2)
         launch(turn + 2)
-        if turn == 0:
-            make_image(6)
-            far_start(6)
-        else:
-            for d in (1, 2, 3):
-                make_part(d)
+        filler()
+        await_all(turn + 2)
+        add_strips(turn + 2)
         for c in range(3):
-            result[c] = ext[c, 2 : X + 2, 0:Y]
-        await_all(turn + 1)
-        put_own(ext, own_p)
-        unpack_halo(turn + 1, ext)
-        image = operate(own_p)
+            for x in range(X):
+                here, there = (c * wide + 2 + x) * 16, (c * X + x) * Y
+                result[there : there + Y, :] = ext[here : here + Y, :]
+        out = operate(ext, result)
         for c in range(3):
-            own_u[c] = current[c] - image[c]
-        result[...] += prolong(first + weight[...] * restrict(own_u))
-        await_all(turn + 2)
-        add_ring(turn + 2, result)
-
-    def image_of(turn, field, result):
-        pack_own(turn, field)
-        launch(turn)
-        put_own(ext, field)
-        if turn == 3:
-            make_image(4)
-            far_start(4)
-            make_image(5)
-            far_start(5)
-            make_image(7)
-        await_all(turn)
-        unpack_halo(turn, ext)
-        out = operate(field)
-        for c in range(3):
-            result[c] = out[c]
-
-    precondition(0, r_ref, own_z)
-    image_of(3, own_z, own_w)
-    pack_own(4, own_w)
-    launch(4)
-    for d in (6, 4, 7):
-        make_part(d)
-    precondition(4, own_w, own_v)
-    image_of(7, own_v, own_u)
+            image[c * per : (c + 1) * per, :] = out[c]
+
+    def fill_images():
+        for d in (6, 4, 5):
+            make_image(d)
+            far_start(d)
+        make_image(7)
+
+    def fill_parts():
+        for d in (6, 4, 7):
+            make_part(d)
+
+    apply_both(0, r_ref, own_z, own_w, fill_images)
+    pack_own(3, own_w)
+    launch(3)
+    apply_both(3, own_w, own_v, own_u, fill_parts)
 
     pairs = ((r_ref, own_z), (own_z, own_w), (r_ref, own_v), (own_w, own_v), (own_z, own_u), (own_v, own_u))
     for i, (a, b) in enumerate(pairs):
-        part = jnp.sum((a[...] * b[...]).reshape(3 * X, Y, Z), axis=0)
+        part = jnp.sum((a[...] * b[...]).reshape(3 * X, 8, Z), axis=0)
         dots[i : i + 1, :] = jnp.sum(part, axis=0, keepdims=True)
 
-    def exchange(axis_pos, me, size, buffer, s_sem, r_sem):
+    def exchange(axis_pos, me, size, buffer, s_sem, r_sem, filler):
         def target(o):
             other = lax.rem(me + o, size)
             return (other, (other, gy) if axis_pos == 0 else (gx, other))
@@ -524,27 +559,18 @@
         for o in range(1, size):
             copy(o, None).start()
         buffer[me] = dots[...]
+        filler()
         for o in range(1, size):
             copy(o, 1).wait_recv()
         for o in range(1, size):
             copy(o, None).wait_send()
         dots[...] = jnp.sum(buffer[...], axis=0)
 
-    exchange(0, gx, n_gx, sums_x, sx_send, sx_recv)
-    exchange(1, gy, n_gy, sums_y, sy_send, sy_recv)
-    total = jnp.sum(dots[...], axis=1, keepdims=True)
-    rz, zw, rv, wv, zu, vu = (total[i : i + 1, :] for i in range(6))
-    step0 = rz / zw
-    rz_new = step0 * (step0 * wv - rv)
-    grow = 1.0 + rz_new / rz
-    step1 = rz_new / (grow * grow * zw - grow * step0 * (wv + zu) + step0 * step0 * vu)
-    keep = jnp.broadcast_to(step0 + step1 * grow, (Y, Z))[None, None]
-    cross = jnp.broadcast_to(step1 * step0, (Y, Z))[None, None]
-    x_out[...] = keep * own_z[...] - cross * own_v[...]
-    res_out[...] = r_ref[...] - keep * own_w[...] + cross * own_u[...]
-
-    for d in range(8):
-
+    def later_parts():
+        for d in (1, 3, 2):
+            make_part(d)
+
+    def finish(d):
         @pl.when(exists(d))
         def _():
             whole = share[d] if d in (2, 7) else None
@@ -552,11 +578,35 @@
                 part_arrival(d).wait_recv()
                 whole = share_far[d] if d in (0, 5) else share[d] + share_far[d]
             tile = jnp.concatenate([whole[:, 0:K], whole[:, K : 2 * K]], axis=0)
-            tile_out[d] = tile if d >= 4 else tile.T
+            square[:, 0:K] = tile if d >= 4 else tile.T
+            even = square[pl.ds(0, K // 2, stride=2), :]
+            odd = square[pl.ds(1, K // 2, stride=2), :]
+            packed[d * K // 2 : (d + 1) * K // 2, :] = jnp.concatenate([even[:, 0:K], odd[:, 0:K]], axis=1)
 
         @pl.when(jnp.logical_not(exists(d)))
         def _():
-            tile_out[d] = jnp.zeros((K, K), jnp.float32)
+            packed[d * K // 2 : (d + 1) * K // 2, :] = jnp.zeros((K // 2, 2 * K), jnp.float32)
+
+    def early_tiles():
+        for d in (7, 2):
+            finish(d)
+
+    exchange(0, gx, n_gx, sums_x, sx_send, sx_recv, later_parts)
+    exchange(1, gy, n_gy, sums_y, sy_send, sy_recv, early_tiles)
+    total = jnp.sum(dots[...], axis=1, keepdims=True)
+    rz, zw, rv, wv, zu, vu = (total[i : i + 1, :] for i in range(6))
+    step0 = rz / zw
+    rz_new = step0 * (step0 * wv - rv)
+    grow = 1.0 + rz_new / rz
+    step1 = rz_new / (grow * grow * zw - grow * step0 * (wv + zu) + step0 * step0 * vu)
+    keep = step0 + step1 * grow
+    cross = step1 * step0
+    x_out[...] = keep * own_z[...] - cross * own_v[...]
+    res_out[...] = r_ref[...] - keep * own_w[...] + cross * own_u[...]
+    for d in (0, 5, 4, 6, 3, 1):
+        finish(d)
+    for j in range(K // 2):
+        tile_out[:, j * 2 * K : (j + 1) * 2 * K] = packed[pl.ds(j, 8, stride=K // 2), :]
 
     for d in range(8):
 
@@ -570,26 +620,39 @@
                 message(turn, d).wait_send()
 
 
+def emit(*refs):
+    sems = refs[6]
+    copies = [pltpu.make_async_copy(refs[i], refs[3 + i], sems.at[i]) for i in range(3)]
+    for copy in copies:
+        copy.start()
+    for copy in copies:
+        copy.wait()
+
+
 def per_device(n_gx, n_gy, right_side, stiffness, panels):
     X, Y, Z = stiffness.shape
     K = panels.shape[0]
     f32 = jnp.float32
-    field = pltpu.VMEM((3, X, Y, Z), f32)
+    cells = 3 * X * Y
+    field = pltpu.VMEM((cells, Z), f32)
+    padded = pltpu.VMEM((3 * (X + 4) * 16, Z), f32)
     dma = pltpu.SemaphoreType.DMA
     vmem = pl.BlockSpec(memory_space=pltpu.VMEM)
-    x, res, tiles = pl.pallas_call(
+    anywhere = pl.BlockSpec(memory_space=pltpu.HBM)
+    results = (
+        jax.ShapeDtypeStruct((cells, Z), f32),
+        jax.ShapeDtypeStruct((cells, Z), f32),
+        jax.ShapeDtypeStruct((8, K * K), f32),
+    )
+    values = pl.pallas_call(
         functools.partial(kernel, n_gx, n_gy),
-        out_shape=(
-            jax.ShapeDtypeStruct((3, X, Y, Z), f32),
-            jax.ShapeDtypeStruct((3, X, Y, Z), f32),
-            jax.ShapeDtypeStruct((8, K, K), f32),
-        ),
-        in_specs=[pl.BlockSpec(memory_space=pl.ANY)] * 3,
+        out_shape=results,
+        in_specs=[anywhere] * 3,
         out_specs=(vmem,) * 3,
         scratch_shapes=[
             field,
-            pltpu.VMEM((X, Y, Z), f32),
-            pltpu.VMEM((K * 3 * X * Y, Z), f32),
+            pltpu.VMEM((X * Y, Z), f32),
+            pltpu.VMEM((K * cells, Z), f32),
             pltpu.VMEM((3, X, Y, K, Z), f32),
             pltpu.VMEM((2, 3, Y // 2, K, Z), f32),
             pltpu.VMEM((2, 3, X // 2, K, Z), f32),
@@ -599,14 +662,15 @@
             pltpu.VMEM((2, 3, K, Z), f32),
             pltpu.VMEM((8, K // 2, 2 * K), f32),
             pltpu.VMEM((8, K // 2, 2 * K), f32),
-            pltpu.VMEM((ROUNDS, 8, 32, Z), f32),
-            pltpu.VMEM((ROUNDS, 8, 32, Z), f32),
-            pltpu.VMEM((3, X + 4, 16, Z), f32),
-            pltpu.VMEM((3, X + 4, 16, Z), f32),
-            pltpu.VMEM((X + 4, 16, Z), f32),
+            pltpu.VMEM((ROUNDS, 8, 64, Z), f32),
+            pltpu.VMEM((ROUNDS, 8, 64, Z), f32),
+            padded, padded, padded,
+            pltpu.VMEM(((X + 4) * 16, Z), f32),
             field, field, field, field, field,
             pltpu.VMEM((K, Z), f32),
             pltpu.VMEM((K, Z), f32),
+            pltpu.VMEM((K, 2 * K), f32),
+            pltpu.VMEM((8 * K // 2, 2 * K), f32),
             pltpu.VMEM((8, Z), f32),
             pltpu.VMEM((n_gx, 8, Z), f32),
             pltpu.VMEM((n_gy, 8, Z), f32),
@@ -616,8 +680,16 @@
         compiler_params=pltpu.CompilerParams(
             collective_id=0, has_side_effects=True, vmem_limit_bytes=56 * 1024 * 1024
         ),
-    )(right_side, stiffness, panels.reshape(K * 3 * X * Y, Z))
-    return x, res, tiles.reshape(1, 1, 8, K * K)
+    )(right_side.reshape(cells, Z), stiffness.reshape(X * Y, Z), panels.reshape(K * cells, Z))
+    x, res, tiles = pl.pallas_call(
+        emit,
+        out_shape=results,
+        in_specs=[anywhere] * 3,
+        out_specs=(anywhere,) * 3,
+        scratch_shapes=[dma((3,))],
+        compiler_params=pltpu.CompilerParams(vmem_limit_bytes=63 * 1024 * 1024),
+    )(*values)
+    return x.reshape(3, X, Y, Z), res.reshape(3, X, Y, Z), tiles.reshape(1, 1, 8, K * K)
 
 
 def solution(mesh):

time: 57.6 us -> 61.6 us (1.069)
  Pallas kernels: 51.5 us -> 60.4 us
  local copies, waits for them, and re-layouts: 4.56 us -> 0 us
    pallas_call x1 -> x2, Pallas kernels: 51.5 us -> 60.4 us  [the longest x1 52.3 us: per_device(): pl.pallas_call(functools.partial(kernel, n_gx, n_gy), out_shape=results,...]
    unnamed x2 -> x0, local copies, waits for them, and re-layouts: 2.84 us -> none
    reshape x1 -> x0, local copies, waits for them, and re-layouts: 1.72 us -> none  [per_device(): return (x, res, tiles.reshape(1, 1, 8, K * K))]
where the time goes in v2:
time: 61.6 us; the launch traced here: 61 us
  Pallas kernels  60.4 us (98%)
  between operations  0.64 us (1%)
    pallas_call x1, Pallas kernels, per_device(): pl.pallas_call(functools.partial(kernel, n_gx, n_gy), out_shape=results,...  52.3 us
    pallas_call x1, Pallas kernels, per_device(): pl.pallas_call(emit, out_shape=results, in_specs=[anywhere] * 3, out_spec...  8.08 us

profile of v2, /device:TPU:3, one launch (start us, length us, event | category | flops | bytes accessed | tf_op | source)
XLA Modules:
  0.0 61.0 jit_solution(3800470567894007452)
XLA Ops:
  0.6 52.3 %shard_map.58 = (f32[96,128]{1,0:T(8,128)}, f32[96,128]{1,0:T(8,128)}, f32[8,4096]{1,0:T(8,128)}) custom-call(f32[96,128]{1,0:T(8,128)} %bitcast.7, f32[32,128]{1,0:T(8,128)} %bitcast.8, f32[6144,128]{1,0:T(8,128)} %bitcast.6), custom_call_target="tpu_custom_call" | custom-call | tf_op jit(solution)/shard_map/pallas_call | solution.py:647
  53.0 8.1 %shard_map.59 = (f32[96,128]{1,0:T(8,128)}, f32[96,128]{1,0:T(8,128)}, f32[8,4096]{1,0:T(8,128)}) custom-call(f32[96,128]{1,0:T(8,128)} %get-tuple-element.9.refs_0_, f32[96,128]{1,0:T(8,128)} %get-tuple-element.10.refs_1_, f32[8,4096]{1,0:T(8,128)} %get-tuple-element.11.refs_2_), custom_call_target="tpu_custom_call" | custom-call | tf_op jit(solution)/shard_map/pallas_call | solution.py:684

commit v3 on v2

--- a/solution.py
+++ b/solution.py
@@ -338,14 +338,23 @@
                 parts = ring_image([panel[c, px, py].reshape(1, K, Z) for c in range(3)], sx, sy)
                 for c in range(3):
                     image_c[0 if d == 5 else 1, c] = parts[c].reshape(K, Z)
-            elif sx:
-                parts = ring_image([panel[c, px] for c in range(3)], sx, sy)
-                for c in range(3):
-                    image_x[c] = parts[c]
             else:
-                parts = ring_image([panel[c, :, py] for c in range(3)], sx, sy)
-                for c in range(3):
-                    image_y[c] = parts[c]
+
+                def body(t, carry):
+                    group = pl.ds(pl.multiple_of(t * 8, 8), 8)
+                    if sx:
+                        edge = [panel[c, px, :, group, :] for c in range(3)]
+                    else:
+                        edge = [panel[c, :, py, group, :] for c in range(3)]
+                    parts = ring_image(edge, sx, sy)
+                    for c in range(3):
+                        if sx:
+                            image_x[c, :, group, :] = parts[c]
+                        else:
+                            image_y[c, :, group, :] = parts[c]
+                    return carry
+
+                lax.fori_loop(0, K // 8, body, 0)
 
     def part_copy(d):
         return pltpu.make_async_remote_copy(
@@ -400,23 +409,40 @@
 
     for d in (1, 3, 0):
         far_start(d)
+    for d in (6, 4, 5):
+        make_image(d)
+        far_start(d)
+    make_image(7)
 
     def diagonal(t, carry):
         first = pl.multiple_of(t * 8, 8)
-        v = [panel[c, :, :, pl.ds(first, 8), :] for c in range(3)]
-        scale = (27.0 + s_ref[...].reshape(X, Y, Z))[:, :, None, :]
-        total = jnp.zeros_like(v[0])
+
+        def at(c, y):
+            return panel[c, :, y, pl.ds(first, 8), :]
+
+        total = jnp.zeros((X, 8, Z), jnp.float32)
         for c in range(3):
-            across = v[c] + shift_lead(v[c], 1, 0) + shift_lead(v[c], -1, 0)
-            across = across + shift_lead(across, 1, 1) + shift_lead(across, -1, 1)
-            total = total + v[c] * (scale * v[c] - across) - 2.0 * shift_z(v[c], 1) * across
-        dz2 = shift_z(v[2], 1) - shift_z(v[2], -1)
-        dy1 = shift_lead(v[1], 1, 1) - shift_lead(v[1], -1, 1)
-        both = dy1 + dz2
-        dx = shift_lead(both, 1, 0) - shift_lead(both, -1, 0)
-        dy = shift_lead(dz2, 1, 1) - shift_lead(dz2, -1, 1)
-        total = total + 2.0 * mixing * (v[0] * dx + v[1] * dy)
-        part = jnp.sum(total.reshape(X * Y, 8, Z), axis=0)
+            sums = [at(c, y) + shift_lead(at(c, y), 1, 0) + shift_lead(at(c, y), -1, 0) for y in range(Y)]
+            for y in range(Y):
+                v, across = at(c, y), sums[y]
+                if y > 0:
+                    across = across + sums[y - 1]
+                if y < Y - 1:
+                    across = across + sums[y + 1]
+                scale = jnp.stack(
+                    [jnp.broadcast_to(27.0 + s_ref[x * Y + y : x * Y + y + 1, :], (8, Z)) for x in range(X)]
+                )
+                total = total + v * (scale * v - across) - 2.0 * shift_z(v, 1) * across
+        dz2 = [shift_z(at(2, y), 1) - shift_z(at(2, y), -1) for y in range(Y)]
+        for y in range(Y):
+            both, dy = dz2[y], jnp.zeros((X, 8, Z), jnp.float32)
+            if y > 0:
+                both, dy = both - at(1, y - 1), dy - dz2[y - 1]
+            if y < Y - 1:
+                both, dy = both + at(1, y + 1), dy + dz2[y + 1]
+            dx = shift_lead(both, 1, 0) - shift_lead(both, -1, 0)
+            total = total + 2.0 * mixing * (at(0, y) * dx + at(1, y) * dy)
+        part = jnp.sum(total, axis=0)
         whole = jnp.sum(part, axis=1, keepdims=True)
         weight[pl.ds(first, 8), :] = jnp.broadcast_to(damping / whole, (8, Z))
         return carry
@@ -520,17 +546,11 @@
         for c in range(3):
             image[c * per : (c + 1) * per, :] = out[c]
 
-    def fill_images():
-        for d in (6, 4, 5):
-            make_image(d)
-            far_start(d)
-        make_image(7)
-
     def fill_parts():
         for d in (6, 4, 7):
             make_part(d)
 
-    apply_both(0, r_ref, own_z, own_w, fill_images)
+    apply_both(0, r_ref, own_z, own_w, lambda: None)
     pack_own(3, own_w)
     launch(3)
     apply_both(3, own_w, own_v, own_u, fill_parts)
@@ -685,7 +705,7 @@
         emit,
         out_shape=results,
         in_specs=[anywhere] * 3,
-        out_specs=(anywhere,) * 3,
+        out_specs=(vmem,) * 3,
         scratch_shapes=[dma((3,))],
         compiler_params=pltpu.CompilerParams(vmem_limit_bytes=63 * 1024 * 1024),
     )(*values)

time: 61.6 us -> 57.6 us (0.935)
  Pallas kernels: 60.4 us -> 56.5 us
    pallas_call x1, Pallas kernels: 8.08 us -> 1.68 us  [per_device(): pl.pallas_call(emit, out_shape=results, in_specs=[anywhere] * 3, out_spec...]
    pallas_call x1, Pallas kernels: 52.3 us -> 54.8 us  [per_device(): pl.pallas_call(functools.partial(kernel, n_gx, n_gy), out_shape=results,...]
where the time goes in v3:
time: 57.6 us; the launch traced here: 57.1 us
  Pallas kernels  56.5 us (98%)
  between operations  0.64 us (1%)
    pallas_call x1, Pallas kernels, per_device(): pl.pallas_call(functools.partial(kernel, n_gx, n_gy), out_shape=results,...  54.8 us
    pallas_call x1, Pallas kernels, per_device(): pl.pallas_call(emit, out_shape=results, in_specs=[anywhere] * 3, out_spec...  1.68 us

profile of v3, /device:TPU:3, one launch (start us, length us, event | category | flops | bytes accessed | tf_op | source)
XLA Modules:
  0.0 57.1 jit_solution(17133192626900485165)
XLA Ops:
  0.6 54.8 %shard_map.58 = (f32[96,128]{1,0:T(8,128)}, f32[96,128]{1,0:T(8,128)}, f32[8,4096]{1,0:T(8,128)}) custom-call(f32[96,128]{1,0:T(8,128)} %bitcast.7, f32[32,128]{1,0:T(8,128)} %bitcast.8, f32[6144,128]{1,0:T(8,128)} %bitcast.6), custom_call_target="tpu_custom_call" | custom-call | tf_op jit(solution)/shard_map/pallas_call | solution.py:667
  55.4 1.7 %shard_map.59 = (f32[96,128]{1,0:T(8,128)}, f32[96,128]{1,0:T(8,128)}, f32[8,4096]{1,0:T(8,128)}) custom-call(f32[96,128]{1,0:T(8,128)} %get-tuple-element.9.refs_0_, f32[96,128]{1,0:T(8,128)} %get-tuple-element.10.refs_1_, f32[8,4096]{1,0:T(8,128)} %get-tuple-element.11.refs_2_), custom_call_target="tpu_custom_call" | custom-call | tf_op jit(solution)/shard_map/pallas_call | solution.py:704

commit v4 on v3

--- a/solution.py
+++ b/solution.py
@@ -301,32 +301,37 @@
 
     hx, hy = X // 2, Y // 2
 
-    def far_copy(d):
+    def pieces(d):
+        return {1: hy, 6: hy, 3: hx, 4: hx}.get(d, 1)
+
+    def far_copy(d, i):
         source, slot = {
-            1: lambda: (panel.at[:, 0, 0:hy], far_x.at[1]),
-            3: lambda: (panel.at[:, 0:hx, 0], far_y.at[1]),
+            1: lambda: (panel.at[:, 0, i], far_x.at[1, :, i]),
+            3: lambda: (panel.at[:, i, 0], far_y.at[1, :, i]),
             0: lambda: (panel.at[:, 0, 0], far_c.at[1]),
-            6: lambda: (image_x.at[:, hy:Y], far_x.at[0]),
-            4: lambda: (image_y.at[:, hx:X], far_y.at[0]),
+            6: lambda: (image_x.at[:, hy + i], far_x.at[0, :, i]),
+            4: lambda: (image_y.at[:, hx + i], far_y.at[0, :, i]),
             5: lambda: (image_c.at[0], far_c.at[0]),
         }[d]()
         return pltpu.make_async_remote_copy(
-            src_ref=source, dst_ref=slot, send_sem=far_send.at[d], recv_sem=far_recv.at[7 - d],
+            src_ref=source, dst_ref=slot, send_sem=far_send.at[d, i], recv_sem=far_recv.at[7 - d, i],
             device_id=peer(d), device_id_type=MESH,
         )
 
-    def far_arrival(d):
-        slot = {6: (far_x, 1), 4: (far_y, 1), 7: (far_c, 1), 1: (far_x, 0), 3: (far_y, 0), 2: (far_c, 0)}[d]
-        here = slot[0].at[slot[1]]
+    def far_arrival(d, i):
+        buffer, side = {6: (far_x, 1), 4: (far_y, 1), 7: (far_c, 1), 1: (far_x, 0), 3: (far_y, 0), 2: (far_c, 0)}[d]
+        here = buffer.at[side] if d in (2, 7) else buffer.at[side, :, i]
         return pltpu.make_async_remote_copy(
-            src_ref=here, dst_ref=here, send_sem=far_send.at[d], recv_sem=far_recv.at[d],
+            src_ref=here, dst_ref=here, send_sem=far_send.at[d, i], recv_sem=far_recv.at[d, i],
             device_id=peer(d), device_id_type=MESH,
         )
 
-    def far_start(d):
-        @pl.when(exists(d))
-        def _():
-            far_copy(d).start()
+    def far_start(*which):
+        for d, i in which:
+
+            @pl.when(exists(d))
+            def _():
+                far_copy(d, i).start()
 
     def make_image(d):
         sx, sy = neighbours[d]
@@ -371,7 +376,8 @@
     def make_part(d):
         @pl.when(exists(d))
         def _():
-            far_arrival(d).wait_recv()
+            for i in range(pieces(d)):
+                far_arrival(d, i).wait_recv()
             left, right = [], []
             for c in range(3):
                 if d == 6:
@@ -407,12 +413,20 @@
             share[d] = jnp.concatenate([tile[0 : K // 2], tile[K // 2 : K]], axis=1)
             part_copy(d).start()
 
-    for d in (1, 3, 0):
-        far_start(d)
-    for d in (6, 4, 5):
+    def together(*groups):
+        return [(d, i) for d, low, high in groups for i in range(low, min(high, pieces(d)))]
+
+    quarter = max(hy // 4, 1)
+    after = {
+        0: together((1, 0, 2 * quarter), (3, 0, hx)),
+        1: together((1, 2 * quarter, 3 * quarter), (6, quarter, 2 * quarter), (4, 0, hx)),
+        2: together((1, 3 * quarter, hy), (6, 2 * quarter, 3 * quarter)),
+        4: together((0, 0, 1), (5, 0, 1), (6, 3 * quarter, hy)),
+    }
+    far_start(*after[0])
+    for d in (6, 4, 5, 7):
         make_image(d)
-        far_start(d)
-    make_image(7)
+    far_start(*together((6, 0, quarter)))
 
     def diagonal(t, carry):
         first = pl.multiple_of(t * 8, 8)
@@ -490,6 +504,7 @@
         own_p[...] = prolong(first)
         pack_own(turn + 1, own_p)
         launch(turn + 1)
+        far_start(*after.get(turn + 1, ()))
         put_own(ext_r, current)
         put_own(ext_p, own_p)
         await_all(turn)
@@ -535,6 +550,7 @@
                 ext[here : here + Y, :] = ext[here : here + Y, :] + own_p[there : there + Y, :]
         pack_strips(turn + 2)
         launch(turn + 2)
+        far_start(*after.get(turn + 2, ()))
         filler()
         await_all(turn + 2)
         add_strips(turn + 2)
@@ -633,7 +649,8 @@
         @pl.when(exists(d))
         def _():
             if d not in (2, 7):
-                far_copy(d).wait_send()
+                for i in range(pieces(d)):
+                    far_copy(d, i).wait_send()
             if d not in (0, 5):
                 part_copy(d).wait_send()
             for turn in range(ROUNDS):
@@ -694,7 +711,7 @@
             pltpu.VMEM((8, Z), f32),
             pltpu.VMEM((n_gx, 8, Z), f32),
             pltpu.VMEM((n_gy, 8, Z), f32),
-            dma((3,)), dma((ROUNDS, 8)), dma((ROUNDS, 8)), dma((8,)), dma((8,)), dma((8,)), dma((8,)),
+            dma((3,)), dma((ROUNDS, 8)), dma((ROUNDS, 8)), dma((8, Y)), dma((8, Y)), dma((8,)), dma((8,)),
             dma((n_gx,)), dma((n_gx,)), dma((n_gy,)), dma((n_gy,)),
         ],
         compiler_params=pltpu.CompilerParams(

time: 57.6 us -> 50.2 us (0.87)
  Pallas kernels: 56.5 us -> 49.2 us
    pallas_call x1, Pallas kernels: 54.8 us -> 47.5 us  [per_device(): pl.pallas_call(functools.partial(kernel, n_gx, n_gy), out_shape=results,...]
where the time goes in v4:
time: 50.2 us; the launch traced here: 49.8 us
  Pallas kernels  49.2 us (98%)
  between operations  0.64 us (1%)
    pallas_call x1, Pallas kernels, per_device(): pl.pallas_call(functools.partial(kernel, n_gx, n_gy), out_shape=results,...  47.5 us
    pallas_call x1, Pallas kernels, per_device(): pl.pallas_call(emit, out_shape=results, in_specs=[anywhere] * 3, out_spec...  1.68 us

profile of v4, /device:TPU:3, one launch (start us, length us, event | category | flops | bytes accessed | tf_op | source)
XLA Modules:
  0.0 49.8 jit_solution(1952986089802152470)
XLA Ops:
  0.6 47.5 %shard_map.58 = (f32[96,128]{1,0:T(8,128)}, f32[96,128]{1,0:T(8,128)}, f32[8,4096]{1,0:T(8,128)}) custom-call(f32[96,128]{1,0:T(8,128)} %bitcast.7, f32[32,128]{1,0:T(8,128)} %bitcast.8, f32[6144,128]{1,0:T(8,128)} %bitcast.6), custom_call_target="tpu_custom_call" | custom-call | tf_op jit(solution)/shard_map/pallas_call | solution.py:684
  48.1 1.7 %shard_map.59 = (f32[96,128]{1,0:T(8,128)}, f32[96,128]{1,0:T(8,128)}, f32[8,4096]{1,0:T(8,128)}) custom-call(f32[96,128]{1,0:T(8,128)} %get-tuple-element.9.refs_0_, f32[96,128]{1,0:T(8,128)} %get-tuple-element.10.refs_1_, f32[8,4096]{1,0:T(8,128)} %get-tuple-element.11.refs_2_), custom_call_target="tpu_custom_call" | custom-call | tf_op jit(solution)/shard_map/pallas_call | solution.py:721

commit v5 on v4

--- a/solution.py
+++ b/solution.py
@@ -133,11 +133,6 @@
     load_s.start()
     load_z.start()
     recv[...] = jnp.zeros_like(recv)
-    ext[...] = jnp.zeros_like(ext)
-    ext_r[...] = jnp.zeros_like(ext_r)
-    ext_p[...] = jnp.zeros_like(ext_p)
-    ext_inv[...] = jnp.zeros_like(ext_inv)
-    dots[...] = jnp.zeros_like(dots)
     barrier = pltpu.get_barrier_semaphore()
     count = jnp.int32(n_gx - 1 + n_gy - 1)
     for o in range(1, n_gx):
@@ -151,6 +146,11 @@
         def _():
             pl.semaphore_signal(barrier, inc=1, device_id=peer(d), device_id_type=MESH)
 
+    ext[...] = jnp.zeros_like(ext)
+    ext_r[...] = jnp.zeros_like(ext_r)
+    ext_p[...] = jnp.zeros_like(ext_p)
+    ext_inv[...] = jnp.zeros_like(ext_inv)
+    dots[...] = jnp.zeros_like(dots)
     load_r.wait()
     load_s.wait()
 
@@ -562,14 +562,17 @@
         for c in range(3):
             image[c * per : (c + 1) * per, :] = out[c]
 
-    def fill_parts():
-        for d in (6, 4, 7):
-            make_part(d)
-
-    apply_both(0, r_ref, own_z, own_w, lambda: None)
+    def parts_of(*which):
+        def fill():
+            for d in which:
+                make_part(d)
+
+        return fill
+
+    apply_both(0, r_ref, own_z, own_w, parts_of(4, 3))
     pack_own(3, own_w)
     launch(3)
-    apply_both(3, own_w, own_v, own_u, fill_parts)
+    apply_both(3, own_w, own_v, own_u, parts_of(6, 7))
 
     pairs = ((r_ref, own_z), (own_z, own_w), (r_ref, own_v), (own_w, own_v), (own_z, own_u), (own_v, own_u))
     for i, (a, b) in enumerate(pairs):
@@ -601,10 +604,6 @@
         for o in range(1, size):
             copy(o, None).wait_send()
         dots[...] = jnp.sum(buffer[...], axis=0)
-
-    def later_parts():
-        for d in (1, 3, 2):
-            make_part(d)
 
     def finish(d):
         @pl.when(exists(d))
@@ -624,10 +623,10 @@
             packed[d * K // 2 : (d + 1) * K // 2, :] = jnp.zeros((K // 2, 2 * K), jnp.float32)
 
     def early_tiles():
-        for d in (7, 2):
+        for d in (7, 2, 0, 4, 3):
             finish(d)
 
-    exchange(0, gx, n_gx, sums_x, sx_send, sx_recv, later_parts)
+    exchange(0, gx, n_gx, sums_x, sx_send, sx_recv, parts_of(1, 2))
     exchange(1, gy, n_gy, sums_y, sy_send, sy_recv, early_tiles)
     total = jnp.sum(dots[...], axis=1, keepdims=True)
     rz, zw, rv, wv, zu, vu = (total[i : i + 1, :] for i in range(6))
@@ -639,7 +638,7 @@
     cross = step1 * step0
     x_out[...] = keep * own_z[...] - cross * own_v[...]
     res_out[...] = r_ref[...] - keep * own_w[...] + cross * own_u[...]
-    for d in (0, 5, 4, 6, 3, 1):
+    for d in (5, 6, 1):
         finish(d)
     for j in range(K // 2):
         tile_out[:, j * 2 * K : (j + 1) * 2 * K] = packed[pl.ds(j, 8, stride=K // 2), :]

time: 50.2 us -> 50 us (level)
  Pallas kernels: 49.2 us -> 48.6 us
    pallas_call x1, Pallas kernels: 47.5 us -> 46.9 us  [per_device(): pl.pallas_call(functools.partial(kernel, n_gx, n_gy), out_shape=results,...]
where the time goes in v5:
time: 50 us; the launch traced here: 49.2 us
  Pallas kernels  48.6 us (97%)
  between operations  0.64 us (1%)
    pallas_call x1, Pallas kernels, per_device(): pl.pallas_call(functools.partial(kernel, n_gx, n_gy), out_shape=results,...  46.9 us
    pallas_call x1, Pallas kernels, per_device(): pl.pallas_call(emit, out_shape=results, in_specs=[anywhere] * 3, out_spec...  1.68 us

profile of v5, /device:TPU:3, one launch (start us, length us, event | category | flops | bytes accessed | tf_op | source)
XLA Modules:
  0.0 49.2 jit_solution(11526688442291985178)
XLA Ops:
  0.6 46.9 %shard_map.58 = (f32[96,128]{1,0:T(8,128)}, f32[96,128]{1,0:T(8,128)}, f32[8,4096]{1,0:T(8,128)}) custom-call(f32[96,128]{1,0:T(8,128)} %bitcast.7, f32[32,128]{1,0:T(8,128)} %bitcast.8, f32[6144,128]{1,0:T(8,128)} %bitcast.6), custom_call_target="tpu_custom_call" | custom-call | tf_op jit(solution)/shard_map/pallas_call | solution.py:683
  47.5 1.7 %shard_map.59 = (f32[96,128]{1,0:T(8,128)}, f32[96,128]{1,0:T(8,128)}, f32[8,4096]{1,0:T(8,128)}) custom-call(f32[96,128]{1,0:T(8,128)} %get-tuple-element.9.refs_0_, f32[96,128]{1,0:T(8,128)} %get-tuple-element.10.refs_1_, f32[8,4096]{1,0:T(8,128)} %get-tuple-element.11.refs_2_), custom_call_target="tpu_custom_call" | custom-call | tf_op jit(solution)/shard_map/pallas_call | solution.py:720
